TPU v7x, 256 devices: a whole 4x4x8 slice. The times are simulated.
256 devices in a mesh: ka: 32 (over z, y), tau: 8 (over x, core).
Axes of the slice: x: 4, y: 4, z: 8, core: 2. Of those that a mesh axis runs over, the one named last changes fastest.
Arguments:
- green: bfloat16 [64, 8, 128, 128], P('ka', 'tau'), may hold values from -6 to 6
- chol: bfloat16 [128, 600, 128, 128], P('ka', 'tau'), may hold values from -0.375 to 0.375
- triplets: int32 [64, 4], replicated, may hold values from 0 to 63, as said below
- diff: int32 [64, 64], replicated, may hold values from 0 to 63, as said below
Outputs:
- sigma: float32 [64, 8, 128, 128], P('ka', 'tau')
Inputs may be any that keep to these rules, and one draw needn't show every extreme that they name: Columns are k1, k2, k3 and owner, a ka index. An owner holds 0 to 4 triplets and some owner holds exactly 4; chol slot owner * 4 + r belongs to that owner's r-th triplet in list order. No two triplets of one owner have k1 // 2 equal. diff[a, b] is the k-point whose lattice vector is that of a minus that of b modulo a mesh of 4 x 4 x 64//16 points; k-points carry permuted labels.
All inputs are finite; a program needn't handle non-finite values.
Results may differ from a plain program's by a relative error of at most 0.0006.
Values may be sent and summed in bfloat16 or wider, within the bound.
A program may use at most 64 MiB of HBM per device.

v0:
```python
import jax
import jax.numpy as jnp
from jax import lax
from jax.sharding import PartitionSpec as P


def aux_block(total):
    best = 1
    for cand in range(1, min(total, 32) + 1):
        if total % cand == 0:
            best = cand
    return best


def on_device(green, chol, triplets, diff):
    per_device = green.shape[0]
    tau_local = green.shape[1]
    orbitals = green.shape[3]
    capacity = chol.shape[0]
    aux_local = chol.shape[1]
    ka_count = lax.axis_size("ka")
    kpoints = per_device * ka_count
    self_index = lax.axis_index("ka")
    owners = triplets[:, 3]
    mine = owners == self_index
    ranks = jnp.cumsum(mine.astype(jnp.int32)) - 1
    slot_match = mine[None, :] & (ranks[None, :] == jnp.arange(capacity, dtype=jnp.int32)[:, None])

    def column(index):
        return jnp.sum(jnp.where(slot_match, triplets[None, :, index], 0), axis=1)

    first = column(0)
    second = column(1)
    third = column(2)
    valid = jnp.any(slot_match, axis=1)
    local_count = jnp.sum(mine.astype(jnp.int32))
    labels = jnp.arange(kpoints, dtype=jnp.int32)

    def lookup(row_ids, col_ids):
        match = (labels[None, :, None] == row_ids[:, None, None]) & (
            labels[None, None, :] == col_ids[:, None, None]
        )
        return jnp.sum(jnp.where(match, diff[None, :, :], 0), axis=(1, 2))

    fourth = lookup(first, lookup(second, third))
    wanted = jnp.where(jnp.concatenate([valid, valid]), jnp.concatenate([second, fourth]), -1)
    piece = lax.all_gather(green, "ka", axis=0, tiled=True)
    place_ids = jnp.arange(piece.shape[0], dtype=jnp.int32)
    select = (wanted[:, None] == place_ids[None, :]).astype(jnp.bfloat16)
    taken = jnp.einsum("ar,rtij->atij", select, piece, preferred_element_type=jnp.float32)
    picked = taken.astype(jnp.bfloat16)
    timeline = lax.all_gather(picked, "tau", axis=1, tiled=True)
    block = aux_block(aux_local)
    groups = chol.reshape(capacity, aux_local // block, block, orbitals, orbitals)

    def one_slot(s, result):
        near = lax.dynamic_index_in_dim(timeline, s, 0, keepdims=False)
        further = lax.dynamic_index_in_dim(timeline, s + capacity, 0, keepdims=False)
        vectors = lax.dynamic_index_in_dim(groups, s, 0, keepdims=False)

        def inner(total, piece):
            product = jnp.einsum("qij,tjl->tqil", piece, near, preferred_element_type=jnp.float32)
            return (total + jnp.einsum("tqil,qil->til", product, piece.astype(jnp.float32)), None)

        summed, unused = lax.scan(
            inner,
            jnp.zeros((tau_local * lax.axis_size("tau"), orbitals, orbitals), jnp.float32),
            vectors,
        )
        term = summed * further.astype(jnp.float32)
        return lax.dynamic_update_index_in_dim(result, term, s, 1)

    zeros = jnp.zeros((tau_local * lax.axis_size("tau"), capacity, orbitals, orbitals), jnp.float32)
    shares = lax.psum_scatter(
        lax.fori_loop(0, local_count, one_slot, zeros), "tau", scatter_dimension=0, tiled=True
    )
    routing = (valid[:, None] & (first[:, None] == labels[None, :])).astype(jnp.float32)
    spread = jnp.einsum("sk,tsij->ktij", routing, shares, precision=lax.Precision.HIGHEST)
    sigma = lax.psum_scatter(spread, "ka", scatter_dimension=0, tiled=True)
    return sigma


def solution(mesh):
    in_specs = (P("ka", "tau", None, None), P("ka", "tau", None, None), P(), P())
    out_specs = P("ka", "tau", None, None)
    return jax.shard_map(
        on_device, mesh=mesh, in_specs=in_specs, out_specs=out_specs, check_vma=False
    )
```

profile of v0, /device:TPU:2, one launch (start us, length us, event | category | flops | bytes accessed | tf_op | source)
XLA Modules:
  0.0 491.7 jit_solution(9981907951954502100)
XLA Ops:
  6.5 0.7 all-gather.4.cloned.1.call-update
  7.3 0.0 all-gather.6.cloned.1.call-start
  7.3 0.7 compare_convert_fusion
  8.0 0.1 copy.20
  8.1 0.1 reduce-window.8
  8.2 0.1 add_reduce_fusion
  8.3 1.3 convert_reduce_fusion
  9.6 0.8 slice_bitcast_fusion.1
  10.4 0.1 select_reduce_fusion.4
  10.6 0.1 reduce_or.9
  10.7 0.1 iota_compare_fusion.1
  10.8 1.0 select_reduce_fusion.1
  11.8 0.1 iota_compare_fusion.3
  11.9 0.1 iota_compare_fusion.4
  11.9 1.0 select_reduce_fusion
  12.9 0.1 add_select_fusion
  13.0 77.9 %all-gather.4.cloned.1.call-done = bf16[64,1,128,128]{3,2,1,0:T(8,128)(2,1)} async-done(((bf16[2,1,128,128]{3,2,1,0:T(8,128)(2,1)}), bf16[64,1,128,128]{3,2,1,0:T(8,128)(2,1)}) %all-gather.4.cloned.1.call-update) | async-done | bytes 2097168 | tf_op jit(solution)/shard_map/all_gather | solution.py:47
  90.9 3.5 fusion.10
  94.5 0.0 all-reduce.3.cloned.1.call-start
  94.5 24.0 %all-gather.6.cloned.1.call-done = bf16[8,1024,128]{2,0,1:T(8,128)(2,1)} async-done(((bf16[8,128,128]{2,0,1:T(8,128)(2,1)}), bf16[8,1024,128]{2,0,1:T(8,128)(2,1)}) %all-gather.6.cloned.1.call-update) | async-done | bytes 2097168 | tf_op jit(solution)/shard_map/all_gather | solution.py:52
  118.5 3.5 copy.22
  122.0 1.5 broadcast_in_dim.81
  123.5 30.7 %while.33 = (s32[]{:T(128)}, f32[8,4,128,128]{3,2,0,1:T(8,128)}, s32[]{:T(128)}, bf16[4,3,25,128,128]{4,3,2,1,0:T(8,128)(2,1)}, bf16[8,8,128,128]{3,2,1,0:T(8,12...) while((s32[]{:T(128)}, f32[8,4,128,128]{3,2,0,1:T(8,128)}, ...), condition=%wide.region_11.12_spmd, body=%wide.region_8.11_spmd.sunk | while | flops 846217216 | bytes 15073677 | solution.py:75
  124.1 1.9 dynamic-slice_bitcast_fusion.5
  126.0 1.7 dynamic-slice_bitcast_fusion.6
  127.7 9.1 %while.34 = (s32[]{:T(128)}, f32[8,128,128]{2,1,0:T(8,128)S(1)}, bf16[3,25,128,128]{3,2,1,0:T(8,128)(2,1)S(1)}, bf16[8,128,128]{2,1,0:T(8,128)(2,1)}, s32[]{:T(128)}, /*index=5*/s32[]{:T(128)}) while((s32[]{:T(128)}, f32[8,128,128]{2,1,0:T(8,128)S(1)}, bf16[3,25,128,128]{3,2,1,0:T(8,128)(2,1)S(1)}, ...), condition=%wide.region_10.10_spmd.clone, body=%wide.region_9.9_spmd.clone.sunk | while | flops 845955072 | bytes 8323187 | solution.py:65
  127.7 0.2 bitcast_convert_fusion.2
  127.8 0.8 copy-done
  128.6 1.9 fusion.31
  130.5 0.2 bitcast_add_fusion.2
  130.7 0.2 bitcast_convert_fusion.2
  130.9 0.7 copy-done
  131.6 1.9 fusion.31
  133.6 0.2 bitcast_add_fusion.2
  133.7 0.2 bitcast_convert_fusion.2
  133.9 0.7 copy-done
  134.7 1.9 fusion.31
  136.6 0.2 bitcast_add_fusion.2
  136.8 1.8 fusion.28
  139.2 1.9 dynamic-slice_bitcast_fusion.5
  141.1 1.7 dynamic-slice_bitcast_fusion.6
  142.7 9.1 %while.34 = (s32[]{:T(128)}, f32[8,128,128]{2,1,0:T(8,128)S(1)}, bf16[3,25,128,128]{3,2,1,0:T(8,128)(2,1)S(1)}, bf16[8,128,128]{2,1,0:T(8,128)(2,1)}, s32[]{:T(128)}, /*index=5*/s32[]{:T(128)}) while((s32[]{:T(128)}, f32[8,128,128]{2,1,0:T(8,128)S(1)}, bf16[3,25,128,128]{3,2,1,0:T(8,128)(2,1)S(1)}, ...), condition=%wide.region_10.10_spmd.clone, body=%wide.region_9.9_spmd.clone.sunk | while | flops 845955072 | bytes 8323187 | solution.py:65
  142.7 0.2 bitcast_convert_fusion.2
  142.9 0.8 copy-done
  143.7 1.9 fusion.31
  145.6 0.2 bitcast_add_fusion.2
  145.8 0.2 bitcast_convert_fusion.2
  146.0 0.7 copy-done
  146.7 1.9 fusion.31
  148.6 0.2 bitcast_add_fusion.2
  148.8 0.2 bitcast_convert_fusion.2
  149.0 0.7 copy-done
  149.7 1.9 fusion.31
  151.6 0.2 bitcast_add_fusion.2
  151.8 1.8 fusion.28
  154.3 0.0 all-reduce.3.cloned.1.call-update
  154.3 0.0 reduce-scatter.5.cloned.1.call-start
  154.3 0.6 copy-done.1
  154.9 0.6 dynamic-slice
  155.5 98.4 %all-reduce.3.cloned.1.call-done = f32[8,4,128,128]{3,2,0,1:T(8,128)} async-done(((f32[8,4,128,128]{3,2,0,1:T(8,128)}), f32[8,4,128,128]{3,2,0,1:T(8,128)}) %all-reduce.3.cloned.1.call-update) | async-done | bytes 2097168
  253.9 1.6 dynamic-slice_bitcast_fusion.2
  255.5 1.9 convolution_bitcast_fusion
  257.4 4.4 copy.24
  261.8 223.4 %reduce-scatter.5.cloned.1.call-done = f32[2,1,128,128]{3,2,1,0:T(8,128)} async-done(((f32[64,1,128,128]{3,2,1,0:T(8,128)}), f32[2,1,128,128]{3,2,1,0:T(8,128)}) %reduce-scatter.5.cloned.1.call-update) | async-done | bytes 131088 | tf_op jit(solution)/shard_map/reduce_scatter | solution.py:79
  (12 shorter events, 0.1 us)
Async XLA Ops:
  6.5 84.4 %all-gather.4.cloned.1.call-start = ((), (), s32[]{:S(2)}) async-start(), calls=%async_computation.1 | async-start | bytes 2162688 | tf_op jit(solution)/shard_map/all_gather | solution.py:47
  7.3 111.3 %all-gather.6.cloned.1.call-start = ((), (), s32[]{:S(2)}) async-start(), calls=%async_computation.3 | async-start | bytes 2359296 | tf_op jit(solution)/shard_map/all_gather | solution.py:52
  94.5 159.4 %all-reduce.3.cloned.1.call-start = ((), (), s32[]{:S(2)}) async-start(), calls=%async_computation.4 | async-start | bytes 4194304
  127.7 0.9 copy-start
  130.7 1.0 copy-start
  133.7 1.0 copy-start
  142.7 0.9 copy-start
  145.8 1.0 copy-start
  148.8 1.0 copy-start
  154.2 0.7 copy-start.1
  154.3 330.9 %reduce-scatter.5.cloned.1.call-start = ((), (), s32[]{:S(2)}) async-start(), calls=%async_computation.2 | async-start | bytes 4325376 | tf_op jit(solution)/shard_map/reduce_scatter | solution.py:79
Sparse Core Ops, SparseCore 0:
  9.9 80.9 all-gather.3
  94.6 23.8 all-gather.5
  154.4 99.4 all-reduce.2
  261.9 223.2 reduce-scatter.4
where the time goes:
time: 493 us; the launch traced here: 492 us
  waiting for transfers between devices  424 us (86%)
  local copies, waits for them, and re-layouts  24.6 us (5%)
  matrix products  16.8 us (3%)
  between operations  13.2 us (3%)
  other arithmetic  10.5 us (2%)
    reduce_scatter x1, waiting for transfers between devices, on_device(): sigma = lax.psum_scatter(spread, 'ka', scatter_dimension=0, tiled=True)  223 us
    unnamed x5, waiting for transfers between devices  99.1 us
    all_gather x1, waiting for transfers between devices, on_device(): piece = lax.all_gather(green, 'ka', axis=0, tiled=True)  77.9 us
    all_gather x1, waiting for transfers between devices, on_device(): timeline = lax.all_gather(picked, 'tau', axis=1, tiled=True)  24 us
    dot_general x6, matrix products, inner(): jnp.einsum('qij,tjl->tqil', piece, near, preferred_element_type=jnp.float32)  11.3 us
  transfers between devices with their start and end apart: 4, of which 4 were waited for; matrix products, arithmetic and copies ran while one was open for 1% of the time, Pallas kernels for 0%

commit v1 on v0

v1 whole, which is shorter than its diff:
```python
import jax
import jax.numpy as jnp
from jax import lax
from jax.experimental import pallas as pl
from jax.experimental.pallas import tpu as pltpu
from jax.sharding import PartitionSpec as P

MESH = pl.DeviceIdType.MESH
ZN, YN, XN, CAP = 8, 4, 4, 4
F32 = jnp.float32
FIRST = (0,)
LAST = (1, 2, 3)
CHUNKS = ((0, 48), (48, 32), (80, 32), (112, 16))
LEVELS = 32766.0
PAIRS = (((0, 0), (1, 0)), ((0, 1), (0, 3)), ((0, 2), (1, 2)), ((1, 1), (1, 3)))


def contract_pair(vectors, near, results, pair, at, step, row):
    x = vectors[:, pl.ds(at, step), :]
    count, _, width = x.shape
    weight = jnp.concatenate([near[e, d] for e, d in pair], axis=1)
    product = jnp.dot(
        x.reshape(count * step, width), weight, preferred_element_type=F32
    ).reshape(count, step, 2 * width)
    wide = x.astype(F32)
    total = jnp.zeros((step, 2 * width), F32)
    for q in range(count):
        total = total + product[q] * jnp.concatenate([wide[q], wide[q]], axis=1)
    for i, (e, d) in enumerate(pair):
        results[e][d, pl.ds(row, step), :] = total[:, i * width : (i + 1) * width]


def kernel(trip_hbm, diff_hbm, green, chol, out, *scratch):
    g = dict(zip(list(SCRATCH), scratch))
    ka = lax.axis_index("ka")
    tau = lax.axis_index("tau")
    z, y = ka // YN, ka % YN
    x, core = tau // 2, tau % 2
    units = [("f%d" % s, (s,), 0, 128) for s in FIRST]
    units += [("c%d" % c, LAST, r0, rows) for c, (r0, rows) in enumerate(CHUNKS)]

    def zdev(d):
        return {"ka": (z + d) % ZN * YN + y}

    def ydev(d):
        return {"ka": z * YN + (y + d) % YN}

    def xdev(d):
        return {"tau": (x + d) % XN * 2 + core}

    sibling = {"tau": x * 2 + 1 - core}

    barrier = pltpu.get_barrier_semaphore()
    peers = [zdev(d) for d in range(1, ZN)] + [ydev(d) for d in range(1, YN)]
    peers += [xdev(d) for d in range(1, XN)] + [sibling]
    for peer in peers:
        pl.semaphore_signal(barrier, inc=1, device_id=peer, device_id_type=MESH)

    ring = [g["ring%d" % d] for d in range(ZN)]
    trip, diff = g["trip"], g["diff"]
    first_loads = [
        pltpu.make_async_copy(green.at[:, 0], ring[0], g["first_sem"].at[0]),
        pltpu.make_async_copy(trip_hbm, trip, g["first_sem"].at[1]),
        pltpu.make_async_copy(diff_hbm, diff, g["first_sem"].at[2]),
    ]
    loads = [
        pltpu.make_async_copy(chol.at[s], g["chol%d" % s], g["chol_sem"].at[s]) for s in range(CAP)
    ]
    for load in first_loads + loads:
        load.start()
    for load in first_loads:
        load.wait()
    pl.semaphore_wait(barrier, len(peers))

    sends = []

    def copy_to(src, dst, name, index, where):
        return pltpu.make_async_remote_copy(
            src_ref=src, dst_ref=dst, send_sem=g[name + "_s"].at[index], recv_sem=g[name + "_r"].at[index],
            device_id=where, device_id_type=MESH,
        )

    def go(*args):
        copy = copy_to(*args)
        copy.start()
        sends.append(copy)

    def hop(way, step, kk):
        if way == 0:
            src, dst, to = ring[step - 1], ring[step], zdev(1)
        else:
            src, dst, to = ring[(ZN + 1 - step) % ZN], ring[ZN - step], zdev(ZN - 1)
        return src.at[kk], dst.at[kk], "ring", (way * ZN + step) * 2 + kk, to

    def hops(step):
        if step < ZN // 2:
            return [(way, step, kk) for kk in range(2) for way in range(2)]
        return [(0, step, 0), (1, step, 1)]

    for args in hops(1):
        go(*hop(*args))

    def scan(t, carry):
        counts, found = carry
        owner = trip[3, t]
        row_hit = (owner // YN) == z
        rel = (owner % YN + YN - y) % YN
        new_counts, new_found = [], []
        for j in range(YN):
            hit = row_hit & (rel == j)
            for s in range(CAP):
                new_found.append(jnp.where(hit & (counts[j] == s), t, found[j * CAP + s]))
            new_counts.append(counts[j] + hit.astype(jnp.int32))
        return tuple(new_counts), tuple(new_found)

    zero = jnp.int32(0)
    state = ((zero,) * YN, (zero,) * (YN * CAP))
    rows_of = trip.shape[1]
    half = ZN // 2
    for step in range(1, half + 1):
        state = lax.fori_loop((step - 1) * rows_of // half, step * rows_of // half, scan, state)
        if step < half:
            ahead = hops(step + 1)
            for way, _, kk in hops(step):
                copy_to(*hop(way, step, kk)).wait_recv()
                if (way, step + 1, kk) in ahead:
                    go(*hop(way, step + 1, kk))
    counts, found = state
    tab = g["tab"]
    firsts = []
    for j in range(YN):
        for s in range(CAP):
            row = found[j * CAP + s]
            k1, k2, k3 = trip[0, row], trip[1, row], trip[2, row]
            for which, k in enumerate((k2, diff[k1, diff[k2, k3]])):
                tab[((j * CAP + s) * 2 + which) * 2] = (z + ZN - k // (2 * YN)) % ZN * 2 + k % 2
                tab[((j * CAP + s) * 2 + which) * 2 + 1] = (y + YN - k // 2 % YN) % YN
            firsts.append(jnp.where(counts[j] > s, k1, -1))
    for way, step, kk in hops(half):
        copy_to(*hop(way, step, kk)).wait_recv()
    pool = g["pool"]
    for d in range(ZN):
        for kk in range(2):
            pool[2 * d + kk] = ring[d][kk]

    def pick(j, s, which):
        return pool[tab[((j * CAP + s) * 2 + which) * 2]]

    def spread(s, which):
        tag = "nf"[which]
        send, recv = g["%ssend%d" % (tag, s)], g["%srecv%d" % (tag, s)]
        for d in range(1, YN):
            send[d - 1] = pick(d, s, which)
            go(send.at[d - 1], recv.at[d], tag, s * YN + d, ydev(d))
        recv[0] = pick(0, s, which)

    def collect(s, which):
        tag = "nf"[which]
        send, recv = g["%ssend%d" % (tag, s)], g["%srecv%d" % (tag, s)]
        for d in range(1, YN):
            copy_to(send.at[d - 1], recv.at[d], tag, s * YN + d, ydev(d)).wait_recv()
        rel = tab[(s * 2 + which) * 2 + 1]
        block = recv[0]
        for d in range(1, YN):
            block = jnp.where(rel == d, recv[d], block)
        return block

    near = [g["near%d" % s] for s in range(CAP)]

    def near_out(s):
        near[s][0, 0] = collect(s, 0)
        go(near[s].at[0, 0], near[s].at[1, 0], "w", s * XN, sibling)
        for d in (1, XN - 1, 2):
            go(near[s].at[0, 0], near[s].at[0, d], "x", s * XN + d, xdev(d))

    def near_on(s):
        for d in (1, XN - 1, 2):
            copy_to(near[s].at[0, 0], near[s].at[0, d], "x", s * XN + d, xdev(d)).wait_recv()
            go(near[s].at[0, d], near[s].at[1, d], "w", s * XN + d, sibling)

    def near_in(s, *ds):
        for d in ds:
            copy_to(near[s].at[0, d], near[s].at[1, d], "w", s * XN + d, sibling).wait_recv()

    def compute(name, s, j, r0, rows, pairs=PAIRS):
        results = [g[k + name].at[:, j] for k in ("keep_", "give_")]
        for pair in pairs:
            for row in range(0, rows, 16):
                contract_pair(g["chol%d" % s], near[s], results, pair, r0 + row, 16, row)

    def sib_out(name):
        go(g["give_" + name], g["sib_" + name], "sib_" + name, 0, sibling)

    def x_out(name):
        keep, sib, sums, recv = (g[k + name] for k in ("keep_", "sib_", "sums_", "xr_"))
        copy_to(g["give_" + name], sib, "sib_" + name, 0, sibling).wait_recv()
        for d in range(1, XN):
            sums[d] = keep[d] + sib[d]
            go(sums.at[d], recv.at[d], "xr_" + name, d, xdev(XN - d))

    def y_out(name, slots, r0, rows):
        keep, sib, sums, recv, own, cand = (
            g[k + name] for k in ("keep_", "sib_", "sums_", "xr_", "own_", "cand_")
        )
        for d in range(1, XN):
            copy_to(sums.at[d], recv.at[d], "xr_" + name, d, xdev(XN - d)).wait_recv()
        for j, s in enumerate(slots):
            total = keep[0, j] + sib[0, j]
            for d in range(1, XN):
                total = total + recv[d, j]
            own[j] = total * g["far%d" % s][pl.ds(r0, rows), :].astype(F32)
        for d in range(1, YN):
            go(own, cand.at[d], "cand_" + name, d, ydev(d))

    def y_in(name):
        for d in range(1, YN):
            copy_to(g["own_" + name], g["cand_" + name].at[d], "cand_" + name, d, ydev(d)).wait_recv()

    route = g["route"]

    def make_routes():
        for dz in range(ZN):
            target = (z + dz) % ZN * YN + y
            for d in range(YN):
                j = (YN - d) % YN
                code = jnp.int32(8)
                for s in range(CAP):
                    k1 = firsts[j * CAP + s]
                    code = jnp.where((k1 >= 0) & ((k1 // 2) == target), s * 2 + k1 % 2, code)
                route[dz * YN + d] = code

    def sums_for(dz, local):
        sums = [jnp.zeros(local.shape[2:], F32) for _ in range(2)]
        for d in range(YN):
            code = route[dz * YN + d]
            block = local[d, (code % 8) // 2]
            for kk in range(2):
                sums[kk] = sums[kk] + jnp.where((code < 8) & (code % 2 == kk), block, 0.0)
        return sums

    def z_out(c):
        name, slots, r0, rows = units[len(FIRST) + c]
        y_in(name)
        local = g["local_" + name]
        for d in range(YN):
            for s in FIRST:
                first = g["own_f%d" % s] if d == 0 else g["cand_f%d" % s].at[d]
                local[d, s] = first[0, pl.ds(r0, rows), :]
            for j, s in enumerate(slots):
                local[d, s] = g["own_" + name][j] if d == 0 else g["cand_" + name][d, j]
        wire, size = g["wireout_" + name], g["sizeout_" + name]
        for dz in range(1, ZN):
            sums = sums_for(dz, local)
            for kk in range(2):
                top = jnp.maximum(jnp.max(jnp.abs(sums[kk]), axis=0, keepdims=True), 1e-30)
                size[dz, pl.ds(kk, 1), :] = top * (1.0 / LEVELS)
                wire[dz, kk] = jnp.round(sums[kk] * (LEVELS / top)).astype(jnp.int32).astype(jnp.int16)
            go(wire.at[dz], g["wire_" + name].at[dz], "wire_" + name, dz, zdev(dz))
            go(size.at[dz], g["size_" + name].at[dz], "size_" + name, dz, zdev(dz))
        sums = sums_for(0, local)
        for kk in range(2):
            out[kk, 0, pl.ds(r0, rows), :] = sums[kk]

    def finish(c):
        name, slots, r0, rows = units[len(FIRST) + c]
        wire, size = g["wire_" + name], g["size_" + name]
        sums = [out[kk, 0, pl.ds(r0, rows), :] for kk in range(2)]
        for dz in range(1, ZN):
            copy_to(g["wireout_" + name].at[dz], wire.at[dz], "wire_" + name, dz, zdev(dz)).wait_recv()
            copy_to(g["sizeout_" + name].at[dz], size.at[dz], "size_" + name, dz, zdev(dz)).wait_recv()
            for kk in range(2):
                scale = size[dz, pl.ds(kk, 1), :]
                sums[kk] = sums[kk] + wire[dz, kk].astype(jnp.int32).astype(F32) * scale
        for kk in range(2):
            out[kk, 0, pl.ds(r0, rows), :] = sums[kk]

    for s in range(CAP):
        spread(s, 0)
        if s == 0:
            near_out(0)
    near_in(0, 0)
    loads[0].wait()
    compute("f0", 0, 0, 0, 128, PAIRS[:1])
    near_on(0)
    near_out(1)
    compute("f0", 0, 0, 0, 128, PAIRS[1:2])
    near_out(2)
    for s in range(CAP):
        spread(s, 1)
    near_in(0, 2)
    compute("f0", 0, 0, 0, 128, PAIRS[2:3])
    near_on(1)
    near_out(3)
    near_in(0, 1, 3)
    compute("f0", 0, 0, 0, 128, PAIRS[3:])
    sib_out("f0")
    near_on(2)
    near_in(1, 0, 1, 2, 3)
    loads[1].wait()
    c0, c1, c2, c3 = units[len(FIRST):]

    def slot(unit, j):
        name, slots, r0, rows = unit
        compute(name, slots[j], j, r0, rows)

    slot(c0, 0)
    near_on(3)
    x_out("f0")
    near_in(2, 0, 1, 2, 3)
    loads[2].wait()
    slot(c0, 1)
    near_in(3, 0, 1, 2, 3)
    loads[3].wait()
    for s in range(CAP):
        g["far%d" % s][...] = collect(s, 1)
    make_routes()
    slot(c0, 2)
    sib_out(c0[0])
    y_out(*units[0])
    slot(c1, 0)
    x_out(c0[0])
    slot(c1, 1)
    slot(c1, 2)
    sib_out(c1[0])
    y_out(*c0)
    y_in("f0")
    slot(c2, 0)
    x_out(c1[0])
    slot(c2, 1)
    z_out(0)
    slot(c2, 2)
    sib_out(c2[0])
    y_out(*c1)
    slot(c3, 0)
    slot(c3, 1)
    x_out(c2[0])
    slot(c3, 2)
    sib_out(c3[0])
    z_out(1)
    y_out(*c2)
    x_out(c3[0])
    finish(0)
    y_out(*c3)
    z_out(2)
    z_out(3)
    finish(1)
    finish(2)
    finish(3)
    for copy in sends:
        copy.wait_send()


SCRATCH = {}


def layout(aux, orb, listed, kpoints):
    dma = pltpu.SemaphoreType.DMA
    spec = {}

    def array(name, dims, dtype):
        spec[name] = pltpu.VMEM(dims, dtype)

    def pair(name, count):
        spec[name + "_s"] = dma((count,))
        spec[name + "_r"] = dma((count,))

    bf = jnp.bfloat16
    spec["trip"] = pltpu.SMEM((4, listed), jnp.int32)
    spec["diff"] = pltpu.SMEM((kpoints, kpoints), jnp.int32)
    spec["first_sem"] = dma((3,))
    spec["chol_sem"] = dma((CAP,))
    for d in range(ZN):
        array("ring%d" % d, (2, orb, orb), bf)
    array("pool", (2 * ZN, orb, orb), bf)
    pair("ring", 4 * ZN)
    for s in range(CAP):
        array("chol%d" % s, (aux, orb, orb), bf)
        for tag in "nf":
            array("%ssend%d" % (tag, s), (YN - 1, orb, orb), bf)
            array("%srecv%d" % (tag, s), (YN, orb, orb), bf)
        array("near%d" % s, (2, XN, orb, orb), bf)
        array("far%d" % s, (orb, orb), bf)
    for tag in "nf":
        pair(tag, CAP * YN)
    pair("x", CAP * XN)
    pair("w", CAP * XN)
    units = [("f%d" % s, 1, orb) for s in FIRST]
    units += [("c%d" % c, len(LAST), rows) for c, (_, rows) in enumerate(CHUNKS)]
    for name, slots, rows in units:
        for kind in ("keep_", "give_", "sib_", "sums_", "xr_"):
            array(kind + name, (XN, slots, rows, orb), F32)
        array("own_" + name, (slots, rows, orb), F32)
        array("cand_" + name, (YN, slots, rows, orb), F32)
        pair("sib_" + name, 1)
        pair("xr_" + name, XN)
        pair("cand_" + name, YN)
        if name[0] == "c":
            array("local_" + name, (YN, CAP, rows, orb), F32)
            for kind in ("wireout_", "wire_"):
                array(kind + name, (ZN, 2, rows, orb), jnp.int16)
            for kind in ("sizeout_", "size_"):
                array(kind + name, (ZN, 8, orb), F32)
            pair("wire_" + name, ZN)
            pair("size_" + name, ZN)
    spec["tab"] = pltpu.SMEM((YN * CAP * 4,), jnp.int32)
    spec["route"] = pltpu.SMEM((ZN * YN,), jnp.int32)
    return spec


def on_device(green, chol, triplets, diff):
    aux, orb = chol.shape[1], chol.shape[3]
    spec = layout(aux, orb, triplets.shape[0], diff.shape[0])
    SCRATCH.clear()
    SCRATCH.update(spec)
    return pl.pallas_call(
        kernel,
        out_shape=jax.ShapeDtypeStruct((2, 1, orb, orb), F32),
        in_specs=[pl.BlockSpec(memory_space=pltpu.HBM)] * 4,
        out_specs=pl.BlockSpec(memory_space=pltpu.VMEM),
        scratch_shapes=list(spec.values()),
        compiler_params=pltpu.CompilerParams(
            collective_id=0, has_side_effects=True, vmem_limit_bytes=64 * 2**20 - 2**17
        ),
    )(triplets.T, diff, green, chol)


def solution(mesh):
    in_specs = (P("ka", "tau", None, None), P("ka", "tau", None, None), P(), P())
    out_specs = P("ka", "tau", None, None)
    return jax.shard_map(
        on_device, mesh=mesh, in_specs=in_specs, out_specs=out_specs, check_vma=False
    )
```

time: 493 us -> 84.5 us (0.17)
  waiting for transfers between devices: 424 us -> 0 us
  Pallas kernels: 0 us -> 82.8 us
  local copies, waits for them, and re-layouts: 24.6 us -> 1.57 us
  matrix products: 16.8 us -> 0 us
  between operations: 13.2 us -> 0.01 us
  other arithmetic: 10.5 us -> 0 us
    reduce_scatter x1 -> x0, waiting for transfers between devices: 223 us -> none  [on_device(): sigma = lax.psum_scatter(spread, 'ka', scatter_dimension=0, tiled=True)]
    all_gather x2 -> x0, waiting for transfers between devices: 102 us -> none  [the longest x1 77.9 us: on_device(): piece = lax.all_gather(green, 'ka', axis=0, tiled=True)]
    unnamed x5 -> x0, waiting for transfers between devices: 99.1 us -> none
    pallas_call x0 -> x1, Pallas kernels: none -> 82.8 us  [on_device(): pl.pallas_call(kernel, out_shape=jax.ShapeDtypeStruct((2, 1, orb, orb), F...]
    dot_general x8 -> x0, matrix products: 16.8 us -> none  [the longest x6 11.3 us: inner(): jnp.einsum('qij,tjl->tqil', piece, near, preferred_element_type=jnp.float32)]
    while x13 -> x0, local copies, waits for them, and re-layouts: 7.98 us -> none
    squeeze x4 -> x0, local copies, waits for them, and re-layouts: 7.04 us -> none  [the longest x2 3.73 us: one_slot(): vectors = lax.dynamic_index_in_dim(groups, s, 0, keepdims=False)]
  transfers between devices with their start and end apart: 4 -> 0, of which waited for: 4 -> 0; matrix products, arithmetic and copies ran while one was open for 1% -> 0% of each run, Pallas kernels for 0% -> 0%
where the time goes in v1:
time: 84.5 us; the launch traced here: 84.4 us
  Pallas kernels  82.8 us (98%)
  local copies, waits for them, and re-layouts  1.57 us (2%)
    pallas_call x1, Pallas kernels, on_device(): pl.pallas_call(kernel, out_shape=jax.ShapeDtypeStruct((2, 1, orb, orb), F...  82.8 us

profile of v1, /device:TPU:2, one launch (start us, length us, event | category | flops | bytes accessed | tf_op | source)
XLA Modules:
  0.0 84.4 jit_solution(3548368733272654547)
XLA Ops:
  0.0 82.8 %shard_map.46 = f32[2,1,128,128]{3,2,1,0:T(8,128)} custom-call(s32[4,64]{1,0:T(4,128)} %bitcast.1, s32[64,64]{1,0:T(8,128)} %diff_hbm.1, bf16[2,1,128,128]{3,2,1,0:T(8,128)(2,1)} %green.1, bf16[4,75,128,128]{3,2,1,0:T(8,128)(2,1)} %chol.1), custom_call_target="tpu_custom_call" | custom-call | tf_op jit(solution)/shard_map/pallas_call | solution.py:415
  82.9 1.6 %copy.6 = f32[2,1,128,128]{3,2,1,0:T(8,128)} copy(f32[2,1,128,128]{3,2,1,0:T(8,128)} %shard_map.46) | data formatting | bytes 262144

commit v2 on v1

--- a/solution.py
+++ b/solution.py
@@ -10,9 +10,21 @@
 F32 = jnp.float32
 FIRST = (0,)
 LAST = (1, 2, 3)
-CHUNKS = ((0, 48), (48, 32), (80, 32), (112, 16))
+CHUNKS = ((0, 32), (32, 32), (64, 32), (96, 16), (112, 16))
 LEVELS = 32766.0
+ZORDER = (4, 3, 5, 2, 6, 1, 7)
 PAIRS = (((0, 0), (1, 0)), ((0, 1), (0, 3)), ((0, 2), (1, 2)), ((1, 1), (1, 3)))
+
+
+def pack(blocks, wire, size, at):
+    for i, block in enumerate(blocks):
+        top = jnp.maximum(jnp.max(jnp.abs(block), axis=0, keepdims=True), 1e-30)
+        size[at, pl.ds(i, 1), :] = top * (1.0 / LEVELS)
+        wire[at, i] = jnp.round(block * (LEVELS / top)).astype(jnp.int32).astype(jnp.int16)
+
+
+def unpack(wire, size, at, i):
+    return wire[at, i].astype(jnp.int32).astype(F32) * size[at, pl.ds(i, 1), :]
 
 
 def contract_pair(vectors, near, results, pair, at, step, row):
@@ -53,9 +65,6 @@
     barrier = pltpu.get_barrier_semaphore()
     peers = [zdev(d) for d in range(1, ZN)] + [ydev(d) for d in range(1, YN)]
     peers += [xdev(d) for d in range(1, XN)] + [sibling]
-    for peer in peers:
-        pl.semaphore_signal(barrier, inc=1, device_id=peer, device_id_type=MESH)
-
     ring = [g["ring%d" % d] for d in range(ZN)]
     trip, diff = g["trip"], g["diff"]
     first_loads = [
@@ -66,6 +75,8 @@
     loads = [
         pltpu.make_async_copy(chol.at[s], g["chol%d" % s], g["chol_sem"].at[s]) for s in range(CAP)
     ]
+    for peer in peers:
+        pl.semaphore_signal(barrier, inc=1, device_id=peer, device_id_type=MESH)
     for load in first_loads + loads:
         load.start()
     for load in first_loads:
@@ -191,30 +202,46 @@
     def sib_out(name):
         go(g["give_" + name], g["sib_" + name], "sib_" + name, 0, sibling)
 
+    def mail(kind, name, src, dst, where):
+        go(g[kind + "wo_" + name].at[src], g[kind + "wi_" + name].at[dst], kind + "w_" + name, dst, where)
+        go(g[kind + "so_" + name].at[src], g[kind + "si_" + name].at[dst], kind + "s_" + name, dst, where)
+
+    def get(kind, name, src, dst, where):
+        copy_to(
+            g[kind + "wo_" + name].at[src], g[kind + "wi_" + name].at[dst], kind + "w_" + name, dst, where
+        ).wait_recv()
+        copy_to(
+            g[kind + "so_" + name].at[src], g[kind + "si_" + name].at[dst], kind + "s_" + name, dst, where
+        ).wait_recv()
+
+    def put(kind, name, src, blocks):
+        pack(blocks, g[kind + "wo_" + name], g[kind + "so_" + name], src)
+
+    def read(kind, name, dst, i):
+        return unpack(g[kind + "wi_" + name], g[kind + "si_" + name], dst, i)
+
     def x_out(name):
-        keep, sib, sums, recv = (g[k + name] for k in ("keep_", "sib_", "sums_", "xr_"))
+        keep, sib = g["keep_" + name], g["sib_" + name]
         copy_to(g["give_" + name], sib, "sib_" + name, 0, sibling).wait_recv()
+        for d in (2, 1, XN - 1):
+            put("x", name, d, [keep[d, j] + sib[d, j] for j in range(keep.shape[1])])
+            mail("x", name, d, d, xdev(XN - d))
+
+    def y_out(name, slots, r0, rows):
+        keep, own = g["keep_" + name], g["own_" + name]
+        totals = [keep[0, j] + g["sib_" + name][0, j] for j in range(len(slots))]
         for d in range(1, XN):
-            sums[d] = keep[d] + sib[d]
-            go(sums.at[d], recv.at[d], "xr_" + name, d, xdev(XN - d))
-
-    def y_out(name, slots, r0, rows):
-        keep, sib, sums, recv, own, cand = (
-            g[k + name] for k in ("keep_", "sib_", "sums_", "xr_", "own_", "cand_")
-        )
-        for d in range(1, XN):
-            copy_to(sums.at[d], recv.at[d], "xr_" + name, d, xdev(XN - d)).wait_recv()
+            get("x", name, d, d, xdev(XN - d))
+            totals = [total + read("x", name, d, j) for j, total in enumerate(totals)]
         for j, s in enumerate(slots):
-            total = keep[0, j] + sib[0, j]
-            for d in range(1, XN):
-                total = total + recv[d, j]
-            own[j] = total * g["far%d" % s][pl.ds(r0, rows), :].astype(F32)
-        for d in range(1, YN):
-            go(own, cand.at[d], "cand_" + name, d, ydev(d))
+            own[j] = totals[j] * g["far%d" % s][pl.ds(r0, rows), :].astype(F32)
+        put("y", name, 0, [own[j] for j in range(len(slots))])
+        for d in (2, 1, YN - 1):
+            mail("y", name, 0, d, ydev(d))
 
     def y_in(name):
         for d in range(1, YN):
-            copy_to(g["own_" + name], g["cand_" + name].at[d], "cand_" + name, d, ydev(d)).wait_recv()
+            get("y", name, 0, d, ydev(d))
 
     route = g["route"]
 
@@ -244,33 +271,28 @@
         local = g["local_" + name]
         for d in range(YN):
             for s in FIRST:
-                first = g["own_f%d" % s] if d == 0 else g["cand_f%d" % s].at[d]
-                local[d, s] = first[0, pl.ds(r0, rows), :]
+                if d == 0:
+                    local[d, s] = g["own_f%d" % s][0, pl.ds(r0, rows), :]
+                else:
+                    scale = g["ysi_f%d" % s][d, pl.ds(0, 1), :]
+                    part = g["ywi_f%d" % s][d, 0, pl.ds(r0, rows), :]
+                    local[d, s] = part.astype(jnp.int32).astype(F32) * scale
             for j, s in enumerate(slots):
-                local[d, s] = g["own_" + name][j] if d == 0 else g["cand_" + name][d, j]
-        wire, size = g["wireout_" + name], g["sizeout_" + name]
-        for dz in range(1, ZN):
-            sums = sums_for(dz, local)
-            for kk in range(2):
-                top = jnp.maximum(jnp.max(jnp.abs(sums[kk]), axis=0, keepdims=True), 1e-30)
-                size[dz, pl.ds(kk, 1), :] = top * (1.0 / LEVELS)
-                wire[dz, kk] = jnp.round(sums[kk] * (LEVELS / top)).astype(jnp.int32).astype(jnp.int16)
-            go(wire.at[dz], g["wire_" + name].at[dz], "wire_" + name, dz, zdev(dz))
-            go(size.at[dz], g["size_" + name].at[dz], "size_" + name, dz, zdev(dz))
+                local[d, s] = g["own_" + name][j] if d == 0 else read("y", name, d, j)
+        for dz in ZORDER:
+            put("z", name, dz, sums_for(dz, local))
+            mail("z", name, dz, dz, zdev(dz))
         sums = sums_for(0, local)
         for kk in range(2):
             out[kk, 0, pl.ds(r0, rows), :] = sums[kk]
 
     def finish(c):
         name, slots, r0, rows = units[len(FIRST) + c]
-        wire, size = g["wire_" + name], g["size_" + name]
         sums = [out[kk, 0, pl.ds(r0, rows), :] for kk in range(2)]
         for dz in range(1, ZN):
-            copy_to(g["wireout_" + name].at[dz], wire.at[dz], "wire_" + name, dz, zdev(dz)).wait_recv()
-            copy_to(g["sizeout_" + name].at[dz], size.at[dz], "size_" + name, dz, zdev(dz)).wait_recv()
+            get("z", name, dz, dz, zdev(dz))
             for kk in range(2):
-                scale = size[dz, pl.ds(kk, 1), :]
-                sums[kk] = sums[kk] + wire[dz, kk].astype(jnp.int32).astype(F32) * scale
+                sums[kk] = sums[kk] + read("z", name, dz, kk)
         for kk in range(2):
             out[kk, 0, pl.ds(r0, rows), :] = sums[kk]
 
@@ -297,11 +319,16 @@
     near_on(2)
     near_in(1, 0, 1, 2, 3)
     loads[1].wait()
-    c0, c1, c2, c3 = units[len(FIRST):]
+    c0, c1, c2, c3, c4 = units[len(FIRST):]
 
     def slot(unit, j):
         name, slots, r0, rows = unit
         compute(name, slots[j], j, r0, rows)
+
+    def end_part(*pairs):
+        name, slots, r0, rows = c4
+        for j, s in enumerate(slots):
+            compute(name, s, j, r0, rows, pairs)
 
     slot(c0, 0)
     near_on(3)
@@ -320,32 +347,38 @@
     slot(c1, 0)
     x_out(c0[0])
     slot(c1, 1)
+    y_in("f0")
     slot(c1, 2)
     sib_out(c1[0])
+    slot(c2, 0)
     y_out(*c0)
-    y_in("f0")
-    slot(c2, 0)
     x_out(c1[0])
     slot(c2, 1)
-    z_out(0)
     slot(c2, 2)
     sib_out(c2[0])
+    z_out(0)
+    slot(c3, 0)
     y_out(*c1)
-    slot(c3, 0)
     slot(c3, 1)
     x_out(c2[0])
     slot(c3, 2)
     sib_out(c3[0])
+    end_part(PAIRS[3], PAIRS[2])
+    x_out(c3[0])
     z_out(1)
+    end_part(PAIRS[0])
+    sib_out(c4[0])
     y_out(*c2)
-    x_out(c3[0])
-    finish(0)
+    end_part(PAIRS[1])
+    x_out(c4[0])
     y_out(*c3)
     z_out(2)
+    finish(0)
+    y_out(*c4)
     z_out(3)
-    finish(1)
-    finish(2)
-    finish(3)
+    z_out(4)
+    for c in range(1, len(CHUNKS)):
+        finish(c)
     for copy in sends:
         copy.wait_send()
 
@@ -387,21 +420,20 @@
     units = [("f%d" % s, 1, orb) for s in FIRST]
     units += [("c%d" % c, len(LAST), rows) for c, (_, rows) in enumerate(CHUNKS)]
     for name, slots, rows in units:
-        for kind in ("keep_", "give_", "sib_", "sums_", "xr_"):
+        for kind in ("keep_", "give_", "sib_"):
             array(kind + name, (XN, slots, rows, orb), F32)
         array("own_" + name, (slots, rows, orb), F32)
-        array("cand_" + name, (YN, slots, rows, orb), F32)
         pair("sib_" + name, 1)
-        pair("xr_" + name, XN)
-        pair("cand_" + name, YN)
+        mails = [("x", XN, slots), ("y", YN, slots)]
         if name[0] == "c":
             array("local_" + name, (YN, CAP, rows, orb), F32)
-            for kind in ("wireout_", "wire_"):
-                array(kind + name, (ZN, 2, rows, orb), jnp.int16)
-            for kind in ("sizeout_", "size_"):
-                array(kind + name, (ZN, 8, orb), F32)
-            pair("wire_" + name, ZN)
-            pair("size_" + name, ZN)
+            mails.append(("z", ZN, 2))
+        for kind, count, blocks in mails:
+            for way in "oi":
+                array(kind + "w" + way + "_" + name, (count, blocks, rows, orb), jnp.int16)
+                array(kind + "s" + way + "_" + name, (count, 4 if blocks > 2 else blocks, orb), F32)
+            pair(kind + "w_" + name, count)
+            pair(kind + "s_" + name, count)
     spec["tab"] = pltpu.SMEM((YN * CAP * 4,), jnp.int32)
     spec["route"] = pltpu.SMEM((ZN * YN,), jnp.int32)
     return spec

time: 84.5 us -> 81 us (0.959)
  Pallas kernels: 82.8 us -> 78.7 us
    pallas_call x1, Pallas kernels: 82.8 us -> 78.7 us  [on_device(): pl.pallas_call(kernel, out_shape=jax.ShapeDtypeStruct((2, 1, orb, orb), F...]
where the time goes in v2:
time: 81 us; the launch traced here: 80.3 us
  Pallas kernels  78.7 us (97%)
  local copies, waits for them, and re-layouts  1.57 us (2%)
    pallas_call x1, Pallas kernels, on_device(): pl.pallas_call(kernel, out_shape=jax.ShapeDtypeStruct((2, 1, orb, orb), F...  78.7 us

profile of v2, /device:TPU:2, one launch (start us, length us, event | category | flops | bytes accessed | tf_op | source)
XLA Modules:
  0.0 80.3 jit_solution(7455532245971443355)
XLA Ops:
  0.0 78.7 %shard_map.46 = f32[2,1,128,128]{3,2,1,0:T(8,128)} custom-call(s32[4,64]{1,0:T(4,128)} %bitcast.1, s32[64,64]{1,0:T(8,128)} %diff_hbm.1, bf16[2,1,128,128]{3,2,1,0:T(8,128)(2,1)} %green.1, bf16[4,75,128,128]{3,2,1,0:T(8,128)(2,1)} %chol.1), custom_call_target="tpu_custom_call" | custom-call | tf_op jit(solution)/shard_map/pallas_call | solution.py:447
  78.7 1.6 %copy.6 = f32[2,1,128,128]{3,2,1,0:T(8,128)} copy(f32[2,1,128,128]{3,2,1,0:T(8,128)} %shard_map.46) | data formatting | bytes 262144

commit v3 on v2

--- a/solution.py
+++ b/solution.py
@@ -75,9 +75,11 @@
     loads = [
         pltpu.make_async_copy(chol.at[s], g["chol%d" % s], g["chol_sem"].at[s]) for s in range(CAP)
     ]
+    for load in first_loads:
+        load.start()
     for peer in peers:
         pl.semaphore_signal(barrier, inc=1, device_id=peer, device_id_type=MESH)
-    for load in first_loads + loads:
+    for load in loads:
         load.start()
     for load in first_loads:
         load.wait()
@@ -96,19 +98,13 @@
         copy.start()
         sends.append(copy)
 
-    def hop(way, step, kk):
-        if way == 0:
-            src, dst, to = ring[step - 1], ring[step], zdev(1)
-        else:
-            src, dst, to = ring[(ZN + 1 - step) % ZN], ring[ZN - step], zdev(ZN - 1)
-        return src.at[kk], dst.at[kk], "ring", (way * ZN + step) * 2 + kk, to
-
-    def hops(step):
-        if step < ZN // 2:
-            return [(way, step, kk) for kk in range(2) for way in range(2)]
-        return [(0, step, 0), (1, step, 1)]
-
-    for args in hops(1):
+    def hop(src, dst, kk):
+        return ring[src].at[kk], ring[dst].at[kk], "ring", dst * 2 + kk, zdev((dst + ZN - src) % ZN)
+
+    near_by = [(0, d, kk) for kk in range(2) for d in (2, ZN - 2)]
+    near_by += [(0, d, kk) for kk in range(2) for d in (1, ZN - 1)]
+    onward = [(2, 3, 0), (2, 4, 0), (ZN - 2, ZN - 3, 0), (2, 3, 1), (ZN - 2, ZN - 3, 1), (ZN - 2, 4, 1)]
+    for args in near_by:
         go(*hop(*args))
 
     def scan(t, carry):
@@ -127,15 +123,13 @@
     zero = jnp.int32(0)
     state = ((zero,) * YN, (zero,) * (YN * CAP))
     rows_of = trip.shape[1]
-    half = ZN // 2
-    for step in range(1, half + 1):
-        state = lax.fori_loop((step - 1) * rows_of // half, step * rows_of // half, scan, state)
-        if step < half:
-            ahead = hops(step + 1)
-            for way, _, kk in hops(step):
-                copy_to(*hop(way, step, kk)).wait_recv()
-                if (way, step + 1, kk) in ahead:
-                    go(*hop(way, step + 1, kk))
+    state = lax.fori_loop(0, rows_of // 2, scan, state)
+    for _, d, kk in near_by[:4]:
+        copy_to(*hop(0, d, kk)).wait_recv()
+        for args in onward:
+            if args[0] == d and args[2] == kk:
+                go(*hop(*args))
+    state = lax.fori_loop(rows_of // 2, rows_of, scan, state)
     counts, found = state
     tab = g["tab"]
     firsts = []
@@ -147,8 +141,8 @@
                 tab[((j * CAP + s) * 2 + which) * 2] = (z + ZN - k // (2 * YN)) % ZN * 2 + k % 2
                 tab[((j * CAP + s) * 2 + which) * 2 + 1] = (y + YN - k // 2 % YN) % YN
             firsts.append(jnp.where(counts[j] > s, k1, -1))
-    for way, step, kk in hops(half):
-        copy_to(*hop(way, step, kk)).wait_recv()
+    for args in near_by[4:] + onward:
+        copy_to(*hop(*args)).wait_recv()
     pool = g["pool"]
     for d in range(ZN):
         for kk in range(2):

time: 81 us -> 76.7 us (0.947)
  Pallas kernels: 78.7 us -> 74.9 us
    pallas_call x1, Pallas kernels: 78.7 us -> 74.9 us  [on_device(): pl.pallas_call(kernel, out_shape=jax.ShapeDtypeStruct((2, 1, orb, orb), F...]
where the time goes in v3:
time: 76.7 us; the launch traced here: 76.5 us
  Pallas kernels  74.9 us (98%)
  local copies, waits for them, and re-layouts  1.57 us (2%)
    pallas_call x1, Pallas kernels, on_device(): pl.pallas_call(kernel, out_shape=jax.ShapeDtypeStruct((2, 1, orb, orb), F...  74.9 us
    unnamed x1, local copies, waits for them, and re-layouts  1.57 us

profile of v3, /device:TPU:2, one launch (start us, length us, event | category | flops | bytes accessed | tf_op | source)
XLA Modules:
  0.0 76.5 jit_solution(4425277477825224930)
XLA Ops:
  0.0 74.9 %shard_map.46 = f32[2,1,128,128]{3,2,1,0:T(8,128)} custom-call(s32[4,64]{1,0:T(4,128)} %bitcast.1, s32[64,64]{1,0:T(8,128)} %diff_hbm.1, bf16[2,1,128,128]{3,2,1,0:T(8,128)(2,1)} %green.1, bf16[4,75,128,128]{3,2,1,0:T(8,128)(2,1)} %chol.1), custom_call_target="tpu_custom_call" | custom-call | tf_op jit(solution)/shard_map/pallas_call | solution.py:441
  74.9 1.6 %copy.6 = f32[2,1,128,128]{3,2,1,0:T(8,128)} copy(f32[2,1,128,128]{3,2,1,0:T(8,128)} %shard_map.46) | data formatting | bytes 262144
